TPU v7x, 32 devices: a whole 2x2x4 slice. The times are simulated.
32 devices in a mesh: row: 8 (over y, x, core), col: 4 (over z).
Axes of the slice: x: 2, y: 2, z: 4, core: 2. Of those that a mesh axis runs over, the one named last changes fastest.
Arguments:
- tiles: bfloat16 [8, 4, 80, 256, 256], P('row', 'col'), may hold values from -0.125 to 0.125
- tile_coords: int32 [2, 8, 4, 80], P(None, 'row', 'col'), may hold values from 0 to 1023, as said below
- tile_counts: int32 [8, 4], P('row', 'col'), may hold values from 40 to 80, as said below
- vectors: bfloat16 [262144, 16], P(('row', 'col')), may hold values from -6 to 6
Outputs:
- product: float32 [262144, 16], P(('row', 'col'))
Inputs may be any that keep to these rules, and one draw needn't show every extreme that they name: `tile_coords`: for slot s below tile_counts[r, c]: the tile row I lies in r * 128 to (r + 1) * 128 - 1; the tile column J has (J // 32) % 4 equal to c; when I != J, I < J exactly when I + J is even; no (row, column) pair appears in two live slots anywhere. Among the live slots of one device at most 35 have tile rows in any one run of 32 tile rows, and at most 28 have tile columns in any one run of 32 tile columns; a device with all slots live reaches both. Slots at or above the count hold 0. `tile_counts`: some device holds exactly 80 live slots.
All inputs are finite; a program needn't handle non-finite values.
Results may differ from a plain program's by a relative error of at most 0.0075.
Values may be sent and summed in bfloat16 or wider, within the bound.
A program may use at most 320 MiB of HBM per device.

v0:
```python
import jax
import jax.numpy as jnp
from jax import lax
from jax.sharding import PartitionSpec as P


def split_tile(stored, tile_rows, tile_cols):
    size_tile = stored.shape[-1]
    down_idx = jnp.arange(size_tile, dtype=jnp.int32)[:, None]
    across_idx = jnp.arange(size_tile, dtype=jnp.int32)[None, :]
    off_diag = (tile_rows != tile_cols)[:, None, None]
    zero_val = jnp.zeros((), stored.dtype)
    upper_part = jnp.where(off_diag | (down_idx <= across_idx)[None], stored, zero_val)
    lower_part = jnp.where(off_diag | (down_idx < across_idx)[None], stored, zero_val)
    return (upper_part, lower_part)


def shards(tiles, tile_coords, tile_counts, vectors):
    size_tile = tiles.shape[-1]
    slot_count = tiles.shape[2]
    vector_width = vectors.shape[1]
    per_slab = vectors.shape[0] // size_tile
    cols_count = lax.axis_size("col")
    row_here = lax.axis_index("row")
    col_here = lax.axis_index("col")
    stored = tiles.reshape(slot_count, size_tile, size_tile)
    tile_rows = tile_coords[0].reshape(slot_count)
    tile_cols = tile_coords[1].reshape(slot_count)
    live_slots = jnp.arange(slot_count, dtype=jnp.int32) < tile_counts.reshape(())
    row_block = lax.all_gather(vectors, "col", axis=0, tiled=True).reshape(
        -1, size_tile, vector_width
    )
    col_group = lax.all_gather(vectors, "row", axis=0, tiled=True).reshape(
        -1, size_tile, vector_width
    )
    row_local = jnp.where(live_slots, tile_rows - row_here * cols_count * per_slab, 0)
    col_local = tile_cols // per_slab // cols_count * per_slab + tile_cols % per_slab
    col_local = jnp.where(live_slots, col_local, 0)
    upper_part, lower_part = split_tile(stored, tile_rows, tile_cols)
    apply_operator = jnp.einsum(
        "tab,tbv->tav", upper_part, col_group[col_local], preferred_element_type=jnp.float32
    ).astype(jnp.bfloat16)
    mirror = jnp.einsum(
        "tba,tbv->tav", lower_part, row_block[row_local], preferred_element_type=jnp.float32
    ).astype(jnp.bfloat16)
    zero_val = jnp.zeros((), jnp.bfloat16)
    apply_operator = jnp.where(live_slots[:, None, None], apply_operator, zero_val).reshape(
        slot_count, size_tile * vector_width
    )
    mirror = jnp.where(live_slots[:, None, None], mirror, zero_val).reshape(
        slot_count, size_tile * vector_width
    )
    local_row_range = per_slab * size_tile
    panel_start = (row_here * cols_count + col_here) * per_slab
    row_targets = jnp.where(live_slots, tile_rows, -1)
    col_targets = jnp.where(live_slots, tile_cols, -1)

    def merge_into_panel(pieces_in):
        products, destination_rows = pieces_in
        wanted = panel_start + jnp.arange(per_slab, dtype=jnp.int32)
        onehot = (destination_rows[:, None] == wanted[None, :]).astype(jnp.bfloat16)
        return jnp.einsum("ts,tk->sk", onehot, products, preferred_element_type=jnp.float32)

    owned_direct = merge_into_panel(
        (
            lax.all_gather(apply_operator, "col", axis=0, tiled=True),
            lax.all_gather(row_targets, "col", axis=0, tiled=True),
        )
    )
    owned_reflected = merge_into_panel(
        (
            lax.all_gather(mirror, "row", axis=0, tiled=True),
            lax.all_gather(col_targets, "row", axis=0, tiled=True),
        )
    )
    owned_direct = owned_direct.reshape(local_row_range, vector_width)
    owned_reflected = owned_reflected.reshape(local_row_range, vector_width)
    return owned_direct + owned_reflected


def solution(mesh):
    in_specs = (
        P("row", "col", None, None, None),
        P(None, "row", "col", None),
        P("row", "col"),
        P(("row", "col"), None),
    )
    out_specs = P(("row", "col"), None)
    return jax.shard_map(shards, mesh=mesh, in_specs=in_specs, out_specs=out_specs, check_vma=False)
```

profile of v0, /device:TPU:0, one launch (start us, length us, event | category | flops | bytes accessed | tf_op | source)
XLA Modules:
  0.0 183.4 jit_solution(3489110521087887098)
XLA Ops:
  6.5 0.7 all-gather.5.cloned.1.call-update
  7.3 0.0 all-gather.9.cloned.1.call-start
  7.3 0.7 all-gather.9.cloned.1.call-update
  8.0 0.0 all-gather.7.cloned.1.call-start
  8.7 0.7 fusion.23
  9.4 0.7 bitcast_compare_fusion
  10.1 29.8 %all-gather.5.cloned.1.call-done = bf16[65536,16]{0,1:T(8,128)(2,1)} async-done(((bf16[8192,16]{0,1:T(8,128)(2,1)}), bf16[65536,16]{0,1:T(8,128)(2,1)}) %all-gather.5.cloned.1.call-update) | async-done | bytes 2097168 | tf_op jit(solution)/shard_map/all_gather | solution.py:33
  39.9 1.7 copy.25
  41.6 0.6 gather_fusion
  42.3 6.9 %fusion.12 = bf16[80,256,16]{1,2,0:T(8,128)(2,1)S(1)} fusion(bf16[80,256,16]{1,2,0:T(8,128)(2,1)S(1)} %gather_fusion, bf16[1,1,80,256,256]{4,3,2,1,0:T(8,128)(2,1)} %param.4, pred[256,256]{1,0:T(8,128)(4,1)S(1)} %iota_compare_fusion.1, pred[80]{0:T(512)(128)(4,1)S(1)} %get-tuple-element.9, pred[80]{0:T(512)(128)(4,1)S(1)} %get-tuple-element.10), kind=kOutput, calls=%fused_computation.18 | convolution fusion | flops 178913280 | bytes 11862176 | tf_op jit(solution)/shard_map/tab,tbv->tav/dot_general | solution.py:40
  49.2 1.3 copy.15
  50.5 1.3 copy.16
  51.8 0.0 all-gather.7.cloned.1.call-update
  51.8 0.0 all-gather.11.cloned.1.call-start
  51.9 17.5 %all-gather.9.cloned.1.call-done = bf16[32768,16]{0,1:T(8,128)(2,1)} async-done(((bf16[8192,16]{0,1:T(8,128)(2,1)}), bf16[32768,16]{0,1:T(8,128)(2,1)}) %all-gather.9.cloned.1.call-update) | async-done | bytes 1048592 | tf_op jit(solution)/shard_map/all_gather | solution.py:30
  69.4 1.3 copy.26
  70.7 0.6 gather_fusion.1
  71.4 5.6 %fusion.13 = bf16[80,256,16]{1,2,0:T(8,128)(2,1)S(1)} fusion(bf16[80,256,16]{1,2,0:T(8,128)(2,1)S(1)} %gather_fusion.1, bf16[1,1,80,256,256]{4,3,2,1,0:T(8,128)(2,1)} %param.4, pred[256,256]{1,0:T(8,128)(4,1)S(1)} %iota_compare_fusion, pred[80]{0:T(512)(128)(4,1)S(1)} %get-tuple-element.9, pred[80]{0:T(512)(128)(4,1)S(1)} %get-tuple-element.10), kind=kOutput, calls=%fused_computation.19 | convolution fusion | flops 178913280 | bytes 11862176 | tf_op jit(solution)/shard_map/tba,tbv->tav/dot_general | solution.py:43
  77.0 1.3 copy.18
  78.3 1.2 copy.19
  79.5 0.0 all-gather.11.cloned.1.call-update
  79.6 0.7 dynamic-slice
  80.2 0.6 dynamic-slice.1
  82.3 0.1 fusion.24
  82.4 7.9 %all-reduce = s32[320]{0:T(512)S(1)} all-reduce(s32[320]{0:T(512)S(1)} %get-tuple-element.6), channel_id=1, replica_groups=mesh['row'=8,'col'=4] {'col'}, use_global_device_ids=true, to_apply=%add | all-reduce | flops 320 | bytes 2560
  90.3 8.0 %all-reduce.1 = s32[640]{0:T(1024)S(1)} all-reduce(s32[640]{0:T(1024)S(1)} %get-tuple-element.5), channel_id=1, replica_groups=mesh['row'=8,'col'=4] {'row'}, use_global_device_ids=true, to_apply=%add.1 | all-reduce | flops 640 | bytes 5120
  98.3 27.2 %all-gather.7.cloned.1.call-done = bf16[320,4096]{1,0:T(8,128)(2,1)} async-done(((bf16[80,4096]{1,0:T(8,128)(2,1)}), bf16[320,4096]{1,0:T(8,128)(2,1)}) %all-gather.7.cloned.1.call-update) | async-done | bytes 2621456 | tf_op jit(solution)/shard_map/all_gather | solution.py:66
  125.5 2.4 %fusion.17 = f32[32,4096]{1,0:T(8,128)S(1)} fusion(bf16[320,4096]{1,0:T(8,128)(2,1)} %all-gather.7.cloned.1.call-done, s32[32]{0:T(128)S(1)} %iota_add_fusion, s32[320]{0:T(512)S(1)} %all-reduce), kind=kOutput, calls=%fused_computation.26 | convolution fusion | flops 83896320 | bytes 3147136 | tf_op jit(solution)/shard_map/ts,tk->sk/dot_general | solution.py:62
  127.9 39.2 %all-gather.11.cloned.1.call-done = bf16[640,4096]{1,0:T(8,128)(2,1)} async-done(((bf16[80,4096]{1,0:T(8,128)(2,1)}), bf16[640,4096]{1,0:T(8,128)(2,1)}) %all-gather.11.cloned.1.call-update) | async-done | bytes 5242896 | tf_op jit(solution)/shard_map/all_gather | solution.py:72
  167.1 3.5 %convolution_add_fusion = f32[32,4096]{1,0:T(8,128)S(1)} fusion(f32[32,4096]{1,0:T(8,128)S(1)} %fusion.17, bf16[640,4096]{1,0:T(8,128)(2,1)} %all-gather.11.cloned.1.call-done, s32[32]{0:T(128)S(1)} %iota_add_fusion, s32[640]{0:T(1024)S(1)} %all-reduce.1), kind=kOutput, calls=%fused_computation.14 | convolution fusion | flops 167923712 | bytes 6294144 | tf_op jit(solution)/shard_map/ts,tk->sk/dot_general | solution.py:62
  170.6 2.8 %add.96 = f32[8192,16]{1,0:T(8,128)} reshape(f32[32,4096]{1,0:T(8,128)S(1)} %convolution_add_fusion) | data formatting | bytes 1048576 | tf_op jit(solution)/shard_map/add | solution.py:78
  173.4 3.5 %copy.20 = f32[8192,16]{0,1:T(8,128)} copy(f32[8192,16]{1,0:T(8,128)} %add.96) | data formatting | bytes 1048576 | tf_op jit(solution)/shard_map/add | solution.py:78
  (14 shorter events, 0.1 us)
Async XLA Ops:
  6.5 33.4 %all-gather.5.cloned.1.call-start = ((), (), s32[]{:S(2)}) async-start(), calls=%async_computation | async-start | bytes 2359296 | tf_op jit(solution)/shard_map/all_gather | solution.py:33
  7.3 62.2 %all-gather.9.cloned.1.call-start = ((), (), s32[]{:S(2)}) async-start(), calls=%async_computation.2 | async-start | bytes 1310720 | tf_op jit(solution)/shard_map/all_gather | solution.py:30
  8.0 117.5 %all-gather.7.cloned.1.call-start = ((), (), s32[]{:S(2)}) async-start(), calls=%async_computation.1 | async-start | bytes 3276800 | tf_op jit(solution)/shard_map/all_gather | solution.py:66
  51.8 115.3 %all-gather.11.cloned.1.call-start = ((), (), s32[]{:S(2)}) async-start(), calls=%async_computation.3 | async-start | bytes 5898240 | tf_op jit(solution)/shard_map/all_gather | solution.py:72
  71.3 8.2 %copy-start.2 = (u32[32]{0:T(128)S(1)}, u32[32]{0:T(128)}, u32[]{:S(2)}) copy-start(u32[32]{0:T(128)} %constant.65) | copy-start | bytes 388
  71.4 8.9 %copy-start.1 = (u32[32]{0:T(128)S(1)}, u32[32]{0:T(128)}, u32[]{:S(2)}) copy-start(u32[32]{0:T(128)} %constant.70) | copy-start | bytes 388
  71.4 10.9 %copy-start = (s32[2,1,1,80]{3,2,1,0:T(1,128)S(1)}, s32[2,1,1,80]{3,2,1,0:T(1,128)}, u32[]{:S(2)}) copy-start(s32[2,1,1,80]{3,2,1,0:T(1,128)} %param.5) | copy-start | bytes 1924
Sparse Core Ops, SparseCore 0:
  9.3 30.5 all-gather.4
  41.5 27.9 all-gather.8
  71.0 54.4 all-gather.6
  127.2 39.8 all-gather.10
where the time goes:
time: 184 us; the launch traced here: 183 us
  waiting for transfers between devices  115 us (62%)
  matrix products  18.5 us (10%)
  local copies, waits for them, and re-layouts  17 us (9%)
  blocking collectives  15.9 us (9%)
  between operations  15.3 us (8%)
    all_gather x1, waiting for transfers between devices, shards(): lax.all_gather(mirror, 'row', axis=0, tiled=True)  39.2 us
    all_gather x1, waiting for transfers between devices, shards(): lax.all_gather(vectors, 'row', axis=0, tiled=True)  29.8 us
    all_gather x1, waiting for transfers between devices, shards(): lax.all_gather(apply_operator, 'col', axis=0, tiled=True)  27.2 us
    all_gather x1, waiting for transfers between devices, shards(): lax.all_gather(vectors, 'col', axis=0, tiled=True)  17.5 us
    unnamed x2, blocking collectives  15.9 us
    dot_general x1, matrix products, shards(): jnp.einsum('tab,tbv->tav', upper_part, col_group[col_local], preferred_el...  6.91 us
    add x2, local copies, waits for them, and re-layouts, shards(): return owned_direct + owned_reflected  6.27 us
    dot_general x2, matrix products, merge_into_panel(): jnp.einsum('ts,tk->sk', onehot, products, preferred_element_type=jnp.floa...  5.94 us
  transfers between devices with their start and end apart: 4, of which 4 were waited for; matrix products, arithmetic and copies ran while one was open for 15% of the time, Pallas kernels for 0%

commit v1 on v0

--- a/solution.py
+++ b/solution.py
@@ -2,6 +2,27 @@
 import jax.numpy as jnp
 from jax import lax
 from jax.sharding import PartitionSpec as P
+
+
+def ring_gather(array, axis, dim):
+    devices, index, rows = (lax.axis_size(axis), lax.axis_index(axis), array.shape[dim])
+    right = [(i, (i + 1) % devices) for i in range(devices)]
+    left = [(i, (i - 1) % devices) for i in range(devices)]
+    out = jnp.zeros((*array.shape[:dim], devices * rows, *array.shape[dim + 1 :]), array.dtype)
+    out = lax.dynamic_update_slice_in_dim(out, array, index * rows, axis=dim)
+    from_left = from_right = array
+    halfway = devices // 2
+    for step in range(1, halfway + 1):
+        from_left = lax.ppermute(from_left, axis, right)
+        out = lax.dynamic_update_slice_in_dim(
+            out, from_left, (index - step) % devices * rows, axis=dim
+        )
+        if step < devices - halfway:
+            from_right = lax.ppermute(from_right, axis, left)
+            out = lax.dynamic_update_slice_in_dim(
+                out, from_right, (index + step) % devices * rows, axis=dim
+            )
+    return out
 
 
 def split_tile(stored, tile_rows, tile_cols):
@@ -27,9 +48,7 @@
     tile_rows = tile_coords[0].reshape(slot_count)
     tile_cols = tile_coords[1].reshape(slot_count)
     live_slots = jnp.arange(slot_count, dtype=jnp.int32) < tile_counts.reshape(())
-    row_block = lax.all_gather(vectors, "col", axis=0, tiled=True).reshape(
-        -1, size_tile, vector_width
-    )
+    row_block = ring_gather(vectors, "col", 0).reshape(-1, size_tile, vector_width)
     col_group = lax.all_gather(vectors, "row", axis=0, tiled=True).reshape(
         -1, size_tile, vector_width
     )

time: 184 us -> 165 us (0.90)
  waiting for transfers between devices: 115 us -> 93.1 us
  starting transfers between devices: 0.12 us -> 6.72 us
  blocking collectives: 15.9 us -> 13.9 us
    all_gather x1 -> x0, waiting for transfers between devices: 17.5 us -> none  [shards(): lax.all_gather(vectors, 'col', axis=0, tiled=True)]
    ppermute x0 -> x3, waiting for transfers between devices: none -> 8.72 us  [the longest x2 8.72 us: ring_gather(): from_left = lax.ppermute(from_left, axis, right)]
    all_gather x1, waiting for transfers between devices: 27.2 us -> 18.8 us  [shards(): lax.all_gather(apply_operator, 'col', axis=0, tiled=True)]
    ppermute x0 -> x3, starting transfers between devices: none -> 6.64 us  [the longest x1 5.1 us: ring_gather(): from_right = lax.ppermute(from_right, axis, left)]
    all_gather x1, waiting for transfers between devices: 29.8 us -> 25.4 us  [shards(): lax.all_gather(vectors, 'row', axis=0, tiled=True)]
    unnamed x2, blocking collectives: 15.9 us -> 13.9 us
  transfers between devices with their start and end apart: 4 -> 6, of which waited for: 4 -> 4; matrix products, arithmetic and copies ran while one was open for 15% -> 16% of each run, Pallas kernels for 0% -> 0%
where the time goes in v1:
time: 165 us
  waiting for transfers between devices  93.1 us (56%)
  matrix products  18.5 us (11%)
  local copies, waits for them, and re-layouts  15.9 us (10%)
  between operations  15.3 us (9%)
  blocking collectives  13.9 us (8%)
  starting transfers between devices  6.72 us (4%)
    all_gather x1, waiting for transfers between devices, shards(): lax.all_gather(mirror, 'row', axis=0, tiled=True)  39.3 us
    all_gather x1, waiting for transfers between devices, shards(): lax.all_gather(vectors, 'row', axis=0, tiled=True)  25.4 us
    all_gather x1, waiting for transfers between devices, shards(): lax.all_gather(apply_operator, 'col', axis=0, tiled=True)  18.8 us
    unnamed x2, blocking collectives  13.9 us
    ppermute x2, waiting for transfers between devices, ring_gather(): from_left = lax.ppermute(from_left, axis, right)  8.72 us
    dot_general x1, matrix products, shards(): jnp.einsum('tab,tbv->tav', upper_part, col_group[col_local], preferred_el...  6.91 us
    add x2, local copies, waits for them, and re-layouts, shards(): return owned_direct + owned_reflected  6.27 us
    dot_general x2, matrix products, merge_into_panel(): jnp.einsum('ts,tk->sk', onehot, products, preferred_element_type=jnp.floa...  5.94 us
  transfers between devices with their start and end apart: 6, of which 4 were waited for; matrix products, arithmetic and copies ran while one was open for 16% of the time, Pallas kernels for 0%

profile of v1, /device:TPU:0, one launch (start us, length us, event | category | flops | bytes accessed | tf_op | source)
XLA Modules:
  0.0 165.0 jit_solution(10316947326568994016)
XLA Ops:
  6.5 0.7 all-gather.4.cloned.1.call-update
  7.3 0.0 all-gather.6.cloned.1.call-start
  7.3 5.1 %collective-permute-start.1 = (bf16[8192,16]{0,1:T(8,128)(2,1)}, bf16[8192,16]{0,1:T(8,128)(2,1)S(1)}, u32[]{:S(2)}, u32[]{:S(2)}) collective-permute-start(bf16[8192,16]{0,1:T(8,128)(2,1)} %param.7), channel_id=1, source_target_pairs={{0,3},{1,0},{2,1},{3,2},{4,7},{5,4},{6,5},{7,6},{8,11},{9,8},{10,9... | collective-permute-start | bytes 786440 | tf_op jit(solution)/shard_map/ppermute | solution.py:21
  13.1 0.7 fusion.23
  13.8 0.7 bitcast_compare_fusion
  14.5 25.4 %all-gather.4.cloned.1.call-done = bf16[65536,16]{0,1:T(8,128)(2,1)} async-done(((bf16[8192,16]{0,1:T(8,128)(2,1)}), bf16[65536,16]{0,1:T(8,128)(2,1)}) %all-gather.4.cloned.1.call-update) | async-done | bytes 2097168 | tf_op jit(solution)/shard_map/all_gather | solution.py:52
  39.9 1.7 %copy.25 = bf16[2,256,8,256]{3,2,0,1:T(8,128)(2,1)S(1)} copy(bf16[2,256,8,256]{3,2,1,0:T(8,128)(2,1)} %bitcast.73) | data formatting | bytes 4194304 | tf_op jit(solution)/shard_map/reshape | solution.py:52
  41.6 0.6 gather_fusion
  42.3 6.9 %fusion.12 = bf16[80,256,16]{1,2,0:T(8,128)(2,1)S(1)} fusion(bf16[80,256,16]{1,2,0:T(8,128)(2,1)S(1)} %gather_fusion, bf16[1,1,80,256,256]{4,3,2,1,0:T(8,128)(2,1)} %param.4, pred[256,256]{1,0:T(8,128)(4,1)S(1)} %iota_compare_fusion.1, pred[80]{0:T(512)(128)(4,1)S(1)} %get-tuple-element.9, pred[80]{0:T(512)(128)(4,1)S(1)} %get-tuple-element.10), kind=kOutput, calls=%fused_computation.18 | convolution fusion | flops 178913280 | bytes 11862176 | tf_op jit(solution)/shard_map/tab,tbv->tav/dot_general | solution.py:59
  49.2 1.3 copy.15
  50.5 1.2 copy.16
  51.7 0.0 all-gather.6.cloned.1.call-update
  51.7 0.0 all-gather.8.cloned.1.call-start
  51.8 0.1 broadcast_in_dim.48
  52.0 1.5 collective-permute-start.2
  53.6 8.7 %collective-permute-done.2 = bf16[8192,16]{0,1:T(8,128)(2,1)S(1)} collective-permute-done((bf16[8192,16]{0,1:T(8,128)(2,1)S(1)}, bf16[8192,16]{0,1:T(8,128)(2,1)S(1)}, u32[]{:S(2)}, u32[]{:S(2)}) %collective-permute-start.2) | collective-permute-done | bytes 262176 | tf_op jit(solution)/shard_map/ppermute | solution.py:16
  62.4 0.1 copy.26
  62.5 0.6 gather_fusion.1
  63.1 5.6 %fusion.13 = bf16[80,256,16]{1,2,0:T(8,128)(2,1)S(1)} fusion(bf16[80,256,16]{1,2,0:T(8,128)(2,1)S(1)} %gather_fusion.1, bf16[1,1,80,256,256]{4,3,2,1,0:T(8,128)(2,1)} %param.4, pred[256,256]{1,0:T(8,128)(4,1)S(1)} %iota_compare_fusion, pred[80]{0:T(512)(128)(4,1)S(1)} %get-tuple-element.9, pred[80]{0:T(512)(128)(4,1)S(1)} %get-tuple-element.10), kind=kOutput, calls=%fused_computation.19 | convolution fusion | flops 178913280 | bytes 11862176 | tf_op jit(solution)/shard_map/tba,tbv->tav/dot_general | solution.py:62
  68.7 1.3 copy.18
  70.0 1.3 copy.19
  71.3 0.6 dynamic-slice.1
  72.0 0.7 dynamic-slice
  74.0 0.1 fusion.24
  74.1 7.2 %all-reduce.1 = s32[640]{0:T(1024)S(1)} all-reduce(s32[640]{0:T(1024)S(1)} %get-tuple-element.5), channel_id=1, replica_groups=mesh['row'=8,'col'=4] {'row'}, use_global_device_ids=true, to_apply=%add.1 | all-reduce | flops 640 | bytes 5120
  81.3 6.7 %all-reduce = s32[320]{0:T(512)S(1)} all-reduce(s32[320]{0:T(512)S(1)} %get-tuple-element.6), channel_id=1, replica_groups=mesh['row'=8,'col'=4] {'col'}, use_global_device_ids=true, to_apply=%add | all-reduce | flops 320 | bytes 2560
  88.0 18.8 %all-gather.6.cloned.1.call-done = bf16[320,4096]{1,0:T(8,128)(2,1)} async-done(((bf16[80,4096]{1,0:T(8,128)(2,1)}), bf16[320,4096]{1,0:T(8,128)(2,1)}) %all-gather.6.cloned.1.call-update) | async-done | bytes 2621456 | tf_op jit(solution)/shard_map/all_gather | solution.py:85
  106.9 2.4 %fusion.17 = f32[32,4096]{1,0:T(8,128)S(1)} fusion(bf16[320,4096]{1,0:T(8,128)(2,1)} %all-gather.6.cloned.1.call-done, s32[32]{0:T(128)S(1)} %iota_add_fusion, s32[320]{0:T(512)S(1)} %all-reduce), kind=kOutput, calls=%fused_computation.26 | convolution fusion | flops 83896320 | bytes 3147136 | tf_op jit(solution)/shard_map/ts,tk->sk/dot_general | solution.py:81
  109.3 39.3 %all-gather.8.cloned.1.call-done = bf16[640,4096]{1,0:T(8,128)(2,1)} async-done(((bf16[80,4096]{1,0:T(8,128)(2,1)}), bf16[640,4096]{1,0:T(8,128)(2,1)}) %all-gather.8.cloned.1.call-update) | async-done | bytes 5242896 | tf_op jit(solution)/shard_map/all_gather | solution.py:91
  148.6 3.5 %convolution_add_fusion = f32[32,4096]{1,0:T(8,128)S(1)} fusion(f32[32,4096]{1,0:T(8,128)S(1)} %fusion.17, bf16[640,4096]{1,0:T(8,128)(2,1)} %all-gather.8.cloned.1.call-done, s32[32]{0:T(128)S(1)} %iota_add_fusion, s32[640]{0:T(1024)S(1)} %all-reduce.1), kind=kOutput, calls=%fused_computation.14 | convolution fusion | flops 167923712 | bytes 6294144 | tf_op jit(solution)/shard_map/ts,tk->sk/dot_general | solution.py:81
  152.2 2.8 %add.131 = f32[8192,16]{1,0:T(8,128)} reshape(f32[32,4096]{1,0:T(8,128)S(1)} %convolution_add_fusion) | data formatting | bytes 1048576 | tf_op jit(solution)/shard_map/add | solution.py:97
  154.9 3.5 %copy.20 = f32[8192,16]{0,1:T(8,128)} copy(f32[8192,16]{1,0:T(8,128)} %add.131) | data formatting | bytes 1048576 | tf_op jit(solution)/shard_map/add | solution.py:97
  (24 shorter events, 0.2 us)
Async XLA Ops:
  6.5 33.4 %all-gather.4.cloned.1.call-start = ((), (), s32[]{:S(2)}) async-start(), calls=%async_computation | async-start | bytes 2359296 | tf_op jit(solution)/shard_map/all_gather | solution.py:52
  7.3 99.6 %all-gather.6.cloned.1.call-start = ((), (), s32[]{:S(2)}) async-start(), calls=%async_computation.1 | async-start | bytes 3276800 | tf_op jit(solution)/shard_map/all_gather | solution.py:85
  7.3 46.3 %collective-permute-start.1 = (bf16[8192,16]{0,1:T(8,128)(2,1)}, bf16[8192,16]{0,1:T(8,128)(2,1)S(1)}, u32[]{:S(2)}, u32[]{:S(2)}) collective-permute-start(bf16[8192,16]{0,1:T(8,128)(2,1)} %param.7), channel_id=1, source_target_pairs={{0,3},{1,0},{2,1},{3,2},{4,7},{5,4},{6,5},{7,6},{8,11},{9,8},{10,9... | collective-permute-start | bytes 786440 | tf_op jit(solution)/shard_map/ppermute | solution.py:21
  12.4 39.6 %collective-permute-start = (bf16[8192,16]{0,1:T(8,128)(2,1)}, bf16[8192,16]{0,1:T(8,128)(2,1)S(1)}, u32[]{:S(2)}, u32[]{:S(2)}) collective-permute-start(bf16[8192,16]{0,1:T(8,128)(2,1)} %param.7), channel_id=1, source_target_pairs={{0,1},{1,2},{2,3},{3,0},{4,5},{5,6},{6,7},{7,4},{8,9},{9,10},{10,1... | collective-permute-start | bytes 786440 | tf_op jit(solution)/shard_map/ppermute | solution.py:16
  49.2 2.7 %copy-start = (bf16[8192,16]{0,1:T(8,128)(2,1)S(1)}, bf16[8192,16]{0,1:T(8,128)(2,1)}, u32[]{:S(2)}) copy-start(bf16[8192,16]{0,1:T(8,128)(2,1)} %param.7) | copy-start | bytes 786436
  51.7 96.9 %all-gather.8.cloned.1.call-start = ((), (), s32[]{:S(2)}) async-start(), calls=%async_computation.2 | async-start | bytes 5898240 | tf_op jit(solution)/shard_map/all_gather | solution.py:91
  52.0 10.3 %collective-permute-start.2 = (bf16[8192,16]{0,1:T(8,128)(2,1)S(1)}, bf16[8192,16]{0,1:T(8,128)(2,1)S(1)}, u32[]{:S(2)}, u32[]{:S(2)}) collective-permute-start(bf16[8192,16]{0,1:T(8,128)(2,1)S(1)} %collective-permute-done), channel_id=1, source_target_pairs={{0,1},{1,2},{2,3},{3,0},{4,5},{5,6},{6,7},{7,4},{8,9},{9,10},{10,1... | collective-permute-start | bytes 786440 | tf_op jit(solution)/shard_map/ppermute | solution.py:16
  63.1 8.3 %copy-start.3 = (u32[32]{0:T(128)S(1)}, u32[32]{0:T(128)}, u32[]{:S(2)}) copy-start(u32[32]{0:T(128)} %constant.97) | copy-start | bytes 388
  63.1 8.9 %copy-start.2 = (u32[32]{0:T(128)S(1)}, u32[32]{0:T(128)}, u32[]{:S(2)}) copy-start(u32[32]{0:T(128)} %constant.92) | copy-start | bytes 388
  63.1 10.9 %copy-start.1 = (s32[2,1,1,80]{3,2,1,0:T(1,128)S(1)}, s32[2,1,1,80]{3,2,1,0:T(1,128)}, u32[]{:S(2)}) copy-start(s32[2,1,1,80]{3,2,1,0:T(1,128)} %param.5) | copy-start | bytes 1924
Sparse Core Ops, SparseCore 0:
  9.3 30.5 all-gather.3
  51.9 54.9 all-gather.5
  108.7 39.8 all-gather.7
